TPU v7x, 512 devices: a whole 4x8x8 slice. The times are simulated.
512 devices in a mesh: sec: 32 (over x, y), term: 16 (over z, core).
Axes of the slice: x: 4, y: 8, z: 8, core: 2. Of those that a mesh axis runs over, the one named last changes fastest.
Arguments:
- vectors: bfloat16 [2, 32, 4, 256, 256], P(None, 'sec'), may hold values from -6 to 6
- left_ops: bfloat16 [48, 32, 256, 256], P('term', 'sec'), may hold values from -0.375 to 0.375
- right_ops: bfloat16 [48, 32, 256, 256], P('term', 'sec'), may hold values from -0.0546875 to 0.0546875
- offsets: int32 [48, 4], P('term'), may hold values from 0 to 31, as said below
Outputs:
- products: bfloat16 [2, 32, 4, 256, 256], P(None, 'sec', None, 'term')
- rayleigh: float32 [2, 2], replicated
Inputs may be any that keep to these rules, and one draw needn't show every extreme that they name: Each term's 4 offsets are distinct, and every shift from 0 to 31 occurs for some term and pair.
All inputs are finite; a program needn't handle non-finite values.
Results may differ from a plain program's by a relative error of at most 0.015.
Values may be sent and summed in bfloat16 or wider, within the bound.
A program may use at most 64 MiB of HBM per device.

v0:
```python
import jax
import jax.numpy as jnp
from jax import lax
from jax.sharding import PartitionSpec as P


def pick_blocks(carried, piece, needed):
    piece_width = piece.shape[1]
    chosen_list = []
    for pair_index in range(needed.shape[1]):
        offset_in = needed[:, pair_index]
        inside = (offset_in >= 0) & (offset_in < piece_width)
        clipped = jnp.clip(offset_in, 0, piece_width - 1)
        candidate = jnp.take_along_axis(piece, clipped[:, None, None, None], axis=1)[:, 0]
        chosen_list.append(jnp.where(inside[:, None, None], candidate, carried[pair_index]))
    return jnp.stack(chosen_list)


def local(vectors, left_ops, right_ops, offsets):
    sectors = lax.axis_size("sec")
    my_sector = lax.axis_index("sec")
    needed = (my_sector + offsets) % sectors
    local_vectors = vectors[:, 0]
    inner_part = jnp.einsum(
        "tab,ipbc->tipac", left_ops[:, 0], local_vectors, preferred_element_type=jnp.float32
    ).astype(jnp.bfloat16)
    pair_count = offsets.shape[1]
    own_right = right_ops[:, 0]
    empty_blocks = jnp.zeros((pair_count,) + own_right.shape, jnp.bfloat16)
    picked = pick_blocks(empty_blocks, lax.all_gather(right_ops, "sec", axis=1, tiled=True), needed)
    partial_value = jnp.einsum(
        "tipac,ptcd->ipad", inner_part, picked, preferred_element_type=jnp.float32
    )
    rows_share = local_vectors.shape[2] // lax.axis_size("term")
    row_start = lax.axis_index("term") * rows_share
    vector_share = lax.dynamic_slice_in_dim(local_vectors, row_start, rows_share, 2).astype(
        jnp.float32
    )
    square_part = jnp.sum(vector_share * vector_share, axis=(1, 2, 3))
    shares = lax.psum_scatter(partial_value, "term", scatter_dimension=2, tiled=True)
    gram_part = jnp.einsum("ipab,jpab->ij", vector_share, shares)
    gram_matrix, squares = lax.psum((gram_part, square_part), ("sec", "term"))
    rayleigh = gram_matrix / jnp.sqrt(squares[:, None] * squares[None, :])
    return (shares.astype(jnp.bfloat16)[:, None], rayleigh)


def solution(mesh):
    in_specs = (
        P(None, "sec", None, None, None),
        P("term", "sec", None, None),
        P("term", "sec", None, None),
        P("term", None),
    )
    out_specs = (P(None, "sec", None, "term", None), P())
    return jax.shard_map(local, mesh=mesh, in_specs=in_specs, out_specs=out_specs, check_vma=False)
```

profile of v0, /device:TPU:1, one launch (start us, length us, event | category | flops | bytes accessed | tf_op | source)
XLA Modules:
  0.0 334.2 jit_solution(14229687823892872018)
XLA Ops:
  7.2 0.7 all-gather.2.cloned.1.call-update
  7.9 1.3 dynamic-slice.1
  9.8 0.7 add_select_fusion
  10.5 0.2 clamp_reduce_fusion.3
  10.8 0.2 and_reduce_fusion.3
  11.1 0.3 multiply_reduce_fusion
  11.4 129.7 %all-gather.2.cloned.1.call-done = bf16[3,32,256,256]{3,2,1,0:T(8,128)(2,1)} async-done(((bf16[3,1,256,256]{3,2,1,0:T(8,128)(2,1)}), bf16[3,32,256,256]{3,2,1,0:T(8,128)(2,1)}) %all-gather.2.cloned.1.call-update) | async-done | bytes 12582928 | tf_op jit(solution)/shard_map/all_gather | solution.py:30
  141.1 5.2 %gather_fusion.3 = bf16[3,256,256]{2,1,0:T(8,128)(2,1)S(1)} fusion(bf16[3,32,256,256]{3,2,1,0:T(8,128)(2,1)} %all-gather.2.cloned.1.call-done, s32[3]{0:T(128)S(1)} %or_bitcast_fusion), kind=kCustom, calls=%fused_computation.3.clone | custom fusion | bytes 786456 | tf_op jit(solution)/shard_map/jit(take_along_axis)/gather | solution.py:14
  146.2 0.2 copy.19
  146.4 5.2 %gather_fusion.2 = bf16[3,256,256]{2,1,0:T(8,128)(2,1)S(1)} fusion(bf16[3,32,256,256]{3,2,1,0:T(8,128)(2,1)} %all-gather.2.cloned.1.call-done, s32[3]{0:T(128)S(1)} %or_bitcast_fusion.1), kind=kCustom, calls=%fused_computation.2.clone | custom fusion | bytes 786456 | tf_op jit(solution)/shard_map/jit(take_along_axis)/gather | solution.py:14
  151.6 0.2 copy.18
  151.7 5.2 %gather_fusion.1 = bf16[3,256,256]{2,1,0:T(8,128)(2,1)S(1)} fusion(bf16[3,32,256,256]{3,2,1,0:T(8,128)(2,1)} %all-gather.2.cloned.1.call-done, s32[3]{0:T(128)S(1)} %or_bitcast_fusion.2), kind=kCustom, calls=%fused_computation.1.clone | custom fusion | bytes 786456 | tf_op jit(solution)/shard_map/jit(take_along_axis)/gather | solution.py:14
  157.0 0.2 copy.17
  157.1 5.2 %gather_fusion = bf16[3,256,256]{2,1,0:T(8,128)(2,1)S(1)} fusion(bf16[3,32,256,256]{3,2,1,0:T(8,128)(2,1)} %all-gather.2.cloned.1.call-done, s32[3]{0:T(128)S(1)} %or_bitcast_fusion.3), kind=kCustom, calls=%fused_computation.clone | custom fusion | bytes 786456 | tf_op jit(solution)/shard_map/jit(take_along_axis)/gather | solution.py:14
  162.3 0.2 copy.16
  162.9 3.2 fusion.5
  166.2 2.2 copy.22
  168.4 59.1 %all-reduce.3 = bf16[2,4,256,256]{3,1,0,2:T(4,128)(2,1)} all-reduce(f32[2,4,256,256]{3,1,0,2:T(4,128)S(1)} %copy.22), channel_id=2, replica_groups=mesh['sec'=32,'term'=16] {'term'}, use_global_device_ids=true, to_apply=%region_0.2.clone | all-reduce | flops 524288 | bytes 3145728
  227.6 0.9 fusion.29
  228.5 0.9 constant_dynamic-slice_fusion
  229.3 0.3 convolution_bitcast_fusion
  229.6 0.7 copy.25
  230.3 96.4 %all-reduce.1 = (f32[2,2]{1,0:T(2,128)S(1)}, f32[2]{0:T(128)S(1)}) all-reduce(f32[2,2]{1,0:T(2,128)S(1)} %convolution_bitcast_fusion, f32[2]{0:T(128)S(1)} %multiply_reduce_fusion), channel_id=1, replica_groups=mesh['sec'=32,'term'=16] {'sec','term'}, use_global_device_ids=true, to_apply=%region_1.3 | all-reduce | flops 6 | bytes 48 | tf_op jit(solution)/shard_map/psum | solution.py:42
  326.7 0.6 rsqrt_multiply_fusion
  (20 shorter events, 0.6 us)
Async XLA Ops:
  7.2 3.9 %copy-start = (bf16[2,1,4,256,256]{4,3,2,1,0:T(8,128)(2,1)S(1)}, bf16[2,1,4,256,256]{4,3,2,1,0:T(8,128)(2,1)}, u32[]{:S(2)}) copy-start(bf16[2,1,4,256,256]{4,3,2,1,0:T(8,128)(2,1)} %param.6) | copy-start | bytes 3145732
  7.2 133.9 %all-gather.2.cloned.1.call-start = ((), (), s32[]{:S(2)}) async-start(), calls=%async_computation | async-start | bytes 12976128 | tf_op jit(solution)/shard_map/all_gather | solution.py:30
  151.7 11.2 %copy-start.1 = (bf16[3,1,256,256]{3,2,1,0:T(8,128)(2,1)S(1)}, bf16[3,1,256,256]{3,2,1,0:T(8,128)(2,1)}, u32[]{:S(2)}) copy-start(bf16[3,1,256,256]{3,2,1,0:T(8,128)(2,1)} %param.7) | copy-start | bytes 1179652
Sparse Core Ops, SparseCore 0:
  11.2 129.8 all-gather.1
where the time goes:
time: 335 us; the launch traced here: 334 us
  blocking collectives  156 us (47%)
  waiting for transfers between devices  130 us (39%)
  local copies, waits for them, and re-layouts  27.3 us (8%)
  between operations  14.9 us (4%)
  matrix products  3.56 us (1%)
    all_gather x1, waiting for transfers between devices, local(): lax.all_gather(right_ops, 'sec', axis=1, tiled=True)  130 us
    psum x1, blocking collectives, local(): gram_matrix, squares = lax.psum((gram_part, square_part), ('sec', 'term'))  96.4 us
    unnamed x1, blocking collectives  59.1 us
    gather x8, local copies, waits for them, and re-layouts, pick_blocks(): jnp.take_along_axis(piece, clipped[:, None, None, None], axis=1)[:, 0]  21.3 us
  transfers between devices with their start and end apart: 1, of which 1 were waited for; matrix products, arithmetic and copies ran while one was open for 1% of the time, Pallas kernels for 0%

commit v1 on v0

v1 whole, which is shorter than its diff:
```python
import functools

import jax
import jax.numpy as jnp
from jax import lax
from jax.experimental import pallas as pl
from jax.experimental.pallas import tpu as pltpu
from jax.sharding import PartitionSpec as P

MESH = pl.DeviceIdType.MESH
X = 4
C = 2
ORDER = (0, 3, 1, 2)


def kernel(Y, Z, off_ref, v_ref, l_ref, rt_ref, prod_ref, ray_ref,
           rg, lg, vg, inner, part, vcol, half, other, zsend, zgot, fin, fgot,
           gx, gk, gz, gy, send, recv):
    NI, PP, B, _ = v_ref.shape
    T = l_ref.shape[0]
    Q = B // X
    PH = PP // C
    sec, term = lax.axis_index("sec"), lax.axis_index("term")
    x, y = sec // Y, sec % Y
    z, k = term // C, term % C

    def at(dx=0, dy=0, dz=0, dk=0):
        return (((x + dx) % X) * Y + (y + dy) % Y, ((z + dz) % Z) * C + (k + dk) % C)

    barrier = pltpu.get_barrier_semaphore()
    peers = [at(dx=d) for d in range(1, X)] + [at(dy=d) for d in range(1, Y)]
    peers += [at(dz=d) for d in range(1, Z)] + [at(dk=1)]
    for peer in peers:
        pl.semaphore_signal(barrier, inc=1, device_id=peer, device_id_type=MESH)
    pl.semaphore_wait(barrier, len(peers))

    started = []

    def copy(src, dst, where):
        n = len(started)
        made = pltpu.make_async_remote_copy(
            src_ref=src, dst_ref=dst, send_sem=send.at[n], recv_sem=recv.at[n],
            device_id=where, device_id_type=MESH)
        made.start()
        started.append(made)
        return made

    rx = {d: copy(rt_ref.at[(x + d) % X], rg.at[0, (-d) % X], at(dx=d)) for d in (1, 3, 2)}
    rg[0, 0] = rt_ref[x]
    ring = {}

    def ring_send(d, j):
        spot = ORDER.index(j)
        for way in (1, -1):
            if 2 * d == Y and (spot < X // 2) != (way == 1):
                continue
            src = rg.at[(-way * (d - 1)) % Y, j]
            ring[d, j, way] = copy(src, rg.at[(-way * d) % Y, j], at(dy=way))

    def ring_pass(d, j):
        for way in (1, -1):
            if (d, j, way) in ring:
                ring[d, j, way].wait_recv()
        if 2 * d < Y:
            ring_send(d + 1, j)

    ring_send(1, 0)
    lx = {1: copy(l_ref, lg.at[3], at(dx=1)), -1: copy(l_ref, lg.at[1], at(dx=-1))}
    mine = pl.ds(k * PH, PH)
    vx = {}
    for first in (0, 1):
        for way in (1, -1):
            i = first if way == 1 else 1 - first
            vx[way, i] = copy(v_ref.at[i, mine], vg.at[(-way) % X, i, mine], at(dx=way))

    def make_inner(o):
        d = ORDER[o]

        def body(n, carry):
            t, p = n // PP, n % PP
            left = l_ref[t] if d == 0 else lg[d, t]
            for i in range(NI):
                v = v_ref[i, p] if d == 0 else vg[d, i, p]
                inner[o, t, p, i * B:(i + 1) * B] = jnp.dot(
                    left, v, preferred_element_type=jnp.float32).astype(jnp.bfloat16)
            return carry

        lax.fori_loop(0, T * PP, body, 0)

    def make_columns(o):
        d = ORDER[o]
        for q in range(X):
            @pl.when(x == q)
            def _():
                for i in range(NI):
                    for p in range(PP):
                        v = v_ref[i, p, :, q * Q:(q + 1) * Q] if d == 0 else vg[d, i, p, :, q * Q:(q + 1) * Q]
                        vcol[o, i, :, :, p * Q:(p + 1) * Q] = v.reshape(Z * C, B // (Z * C), Q)

    make_inner(0)
    for d in (1, 3, 2):
        rx[d].wait_recv()
        ring_send(1, (-d) % X)
    make_columns(0)

    def squares(n, carry):
        rows = pl.ds(pl.multiple_of(n * 16, 16), 16)
        out = []
        for i in range(NI):
            total = carry[i]
            for p in range(PP):
                v = v_ref[i, p, rows].astype(jnp.float32)
                total = total + v * v
            out.append(total)
        return tuple(out)

    zero = jnp.zeros((16, B), jnp.float32)
    square = lax.fori_loop(0, B // 16, squares, (zero,) * NI)

    ring_order = (0, 3, 1, 2) if X == 4 else range(X)
    for j in ring_order:
        ring_pass(1, j)

    hb = B // 2
    vcore, vfwd, lfwd = [], {}, {}
    lx[1].wait_recv()
    lfwd[1] = copy(lg.at[3, :, 0:hb], lg.at[2, :, 0:hb], at(dx=1))
    lx[-1].wait_recv()
    lfwd[-1] = copy(lg.at[1, :, hb:B], lg.at[2, :, hb:B], at(dx=-1))

    def arrived(way, i):
        vx[way, i].wait_recv()
        slot = (-way) % X
        if (way, i) in ((1, 0), (-1, 1)):
            vfwd[way] = copy(vg.at[slot, i, mine], vg.at[2, i, mine], at(dx=way))
        vcore.append(copy(vg.at[slot, i, mine], vg.at[slot, i, mine], at(dk=1)))

    for j in ring_order:
        if 2 * 2 <= Y:
            ring_pass(2, j)
    arrived(1, 0)
    arrived(-1, 1)
    if 2 * 3 <= Y:
        ring_pass(3, 0)
        ring_pass(3, 3)
    arrived(1, 1)
    arrived(-1, 0)
    if 2 * 3 <= Y:
        ring_pass(3, 1)
        ring_pass(3, 2)
    for made in vcore:
        made.wait_recv()
    make_inner(1)
    make_columns(1)
    make_inner(2)
    make_columns(2)
    if 2 * 4 <= Y:
        for j in ring_order:
            ring_pass(4, j)

    def outer(o):
        d = ORDER[o]
        for p in range(PP):
            total = None
            for t in range(T):
                off = off_ref[t, p]
                dy = off % Y
                dx = (d + off // Y + jnp.where(y + dy >= Y, 1, 0)) % X
                here = lax.dot_general(
                    inner[o, t, p], rg[dy, dx, t], (((1,), (1,)), ((), ())),
                    preferred_element_type=jnp.float32)
                total = here if total is None else total + here
            part[o, :, :, :, p * Q:(p + 1) * Q] = total.reshape(NI, Z * C, B // (Z * C), Q)

    swap, zcopy = {}, []

    def swap_send(o):
        for i in range(NI):
            for n in range(Z):
                half[o, i, n] = part[o, i, n * C + 1 - k].astype(jnp.bfloat16)
        swap[o] = copy(half.at[o], other.at[o], at(dk=1))

    def swap_add(o):
        swap[o].wait_recv()
        for i in range(NI):
            for n in range(Z):
                total = part[o, i, n * C + k] + other[o, i, n].astype(jnp.float32)
                zsend[n, o, i] = total.astype(jnp.bfloat16)

    def z_send(first):
        some = pl.ds(first, X // 2)
        for d in range(1, Z):
            zcopy.append(copy(zsend.at[(z + d) % Z, some], zgot.at[d - 1, some], at(dz=d)))

    def gram_add(o, carry):
        def body(n, carry):
            out = list(carry)
            for i in range(NI):
                v = vcol[o, i, n].astype(jnp.float32)
                for j in range(NI):
                    out[i * NI + j] = out[i * NI + j] + v * part[o, j, n]
            return tuple(out)

        return lax.fori_loop(0, Z * C, body, carry)

    gram = (jnp.zeros((B // (Z * C), PP * Q), jnp.float32),) * (NI * NI)
    outer(0)
    swap_send(0)
    outer(1)
    swap_send(1)
    swap_add(0)
    outer(2)
    swap_send(2)
    swap_add(1)
    z_send(0)
    gram = gram_add(0, gram)
    gram = gram_add(1, gram)
    lfwd[1].wait_recv()
    lfwd[-1].wait_recv()
    for way, i in ((1, 0), (-1, 1)):
        vfwd[way].wait_recv()
        vcore.append(copy(vg.at[2, i, mine], vg.at[2, i, mine], at(dk=1)))
    for made in vcore[-2:]:
        made.wait_recv()
    make_inner(3)
    outer(3)
    swap_send(3)
    make_columns(3)
    swap_add(2)
    gram = gram_add(2, gram)
    swap_add(3)
    z_send(X // 2)
    gram = gram_add(3, gram)

    rows = [jnp.sum(g, axis=0, keepdims=True) for g in gram]
    rows += [jnp.sum(s, axis=0, keepdims=True) * (1.0 / (Z * C)) for s in square]
    W = rows[0].shape[1] // 2
    rows = [r[:, :W] + r[:, W:] for r in rows]
    for n, r in enumerate(rows):
        gx[x, n:n + 1] = r
    for n in range(len(rows), 8):
        gx[x, n:n + 1] = jnp.zeros_like(rows[0])

    def spread(buf, me, size, name):
        return [copy(buf.at[me], buf.at[me], at(**{name: d})) for d in range(1, size)]

    def total(buf, copies, size):
        for made in copies:
            made.wait_recv()
        out = buf[0]
        for n in range(1, size):
            out = out + buf[n]
        return out

    got = total(gx, spread(gx, x, X, "dx"), X)
    gk[k] = got
    got = total(gk, spread(gk, k, C, "dk"), C)
    gy[y] = got
    ycopies = spread(gy, y, Y, "dy")

    for made in zcopy:
        made.wait_recv()
    for o in range(X):
        for i in range(NI):
            total_block = zsend[z, o, i].astype(jnp.float32)
            for d in range(Z - 1):
                total_block = total_block + zgot[d, o, i].astype(jnp.float32)
            fin[o, i] = total_block.astype(jnp.bfloat16)
    fcopy = [copy(fin.at[o], fgot.at[x], at(dx=ORDER[o])) for o in range(1, X)]
    fgot[x] = fin[0]
    gz[z] = total(gy, ycopies, Y)
    zcopies = spread(gz, z, Z, "dz")
    for made in fcopy:
        made.wait_recv()
    for q in range(X):
        for i in range(NI):
            for p in range(PP):
                prod_ref[i, p, :, q * Q:(q + 1) * Q] = fgot[q, i, :, p * Q:(p + 1) * Q]
    got = jnp.sum(total(gz, zcopies, Z), axis=1, keepdims=True)
    for i in range(NI):
        for j in range(NI):
            a = got[NI * NI + i:NI * NI + i + 1]
            b = got[NI * NI + j:NI * NI + j + 1]
            n = i * NI + j
            ray_ref[i:i + 1, j:j + 1] = got[n:n + 1] / jnp.sqrt(a * b)
    for made in started:
        made.wait_send()
    assert len(started) <= send.shape[0]


def local(Y, Z, vectors, left_ops, right_ops, offsets):
    NI, _, PP, B, _ = vectors.shape
    T = left_ops.shape[0]
    Q, R = B // X, B // (Z * C)
    turned = right_ops[:, 0].transpose(2, 0, 1).reshape(X, Q, T, B).transpose(0, 2, 1, 3)
    bf, f32 = jnp.bfloat16, jnp.float32
    vmem = pltpu.VMEM
    W = PP * Q
    whole = pl.BlockSpec(memory_space=pltpu.VMEM)
    copies = 96 if Y == 8 else 96
    products, rayleigh = pl.pallas_call(
        functools.partial(kernel, Y, Z),
        out_shape=(jax.ShapeDtypeStruct((NI, PP, R, B), bf), jax.ShapeDtypeStruct((NI, NI), f32)),
        in_specs=[pl.BlockSpec(memory_space=pltpu.SMEM), whole, whole, whole],
        out_specs=(whole, whole),
        scratch_shapes=[
            vmem((Y, X, T, Q, B), bf),
            vmem((X, T, B, B), bf),
            vmem((X, NI, PP, B, B), bf),
            vmem((X, T, PP, NI * B, B), bf),
            vmem((X, NI, Z * C, R, W), f32),
            vmem((X, NI, Z * C, R, W), bf),
            vmem((X, NI, Z, R, W), bf),
            vmem((X, NI, Z, R, W), bf),
            vmem((Z, X, NI, R, W), bf),
            vmem((Z - 1, X, NI, R, W), bf),
            vmem((X, NI, R, W), bf),
            vmem((X, NI, R, W), bf),
            vmem((X, 8, W // 2), f32),
            vmem((C, 8, W // 2), f32),
            vmem((Z, 8, W // 2), f32),
            vmem((Y, 8, W // 2), f32),
            pltpu.SemaphoreType.DMA((copies,)),
            pltpu.SemaphoreType.DMA((copies,)),
        ],
        compiler_params=pltpu.CompilerParams(
            collective_id=0, has_side_effects=True, vmem_limit_bytes=52 * 1024 * 1024),
    )(offsets, vectors[:, 0], left_ops[:, 0], turned)
    return products[:, None], rayleigh


def solution(mesh):
    sectors, terms = mesh.shape["sec"], mesh.shape["term"]
    in_specs = (
        P(None, "sec", None, None, None),
        P("term", "sec", None, None),
        P("term", "sec", None, None),
        P("term", None),
    )
    out_specs = (P(None, "sec", None, "term", None), P())
    return jax.shard_map(
        functools.partial(local, sectors // X, terms // C),
        mesh=mesh, in_specs=in_specs, out_specs=out_specs, check_vma=False)
```

time: 335 us -> 81.3 us (0.24)
  blocking collectives: 156 us -> 0 us
  waiting for transfers between devices: 130 us -> 0 us
  Pallas kernels: 0 us -> 77 us
  local copies, waits for them, and re-layouts: 27.3 us -> 3.44 us
  between operations: 14.9 us -> 0.68 us
  matrix products: 3.56 us -> 0 us
    all_gather x1 -> x0, waiting for transfers between devices: 130 us -> none  [local(): lax.all_gather(right_ops, 'sec', axis=1, tiled=True)]
    psum x1 -> x0, blocking collectives: 96.4 us -> none  [local(): gram_matrix, squares = lax.psum((gram_part, square_part), ('sec', 'term'))]
    pallas_call x0 -> x1, Pallas kernels: none -> 77 us  [local(): pl.pallas_call(functools.partial(kernel, Y, Z), out_shape=(jax.ShapeDtype...]
    unnamed x1 -> x0, blocking collectives: 59.1 us -> none
    gather x8 -> x0, local copies, waits for them, and re-layouts: 21.3 us -> none  [pick_blocks(): jnp.take_along_axis(piece, clipped[:, None, None, None], axis=1)[:, 0]]
    dot_general x2 -> x0, matrix products: 3.56 us -> none  [the longest x1 3.24 us: local(): jnp.einsum('tipac,ptcd->ipad', inner_part, picked, preferred_element_type...]
  transfers between devices with their start and end apart: 1 -> 0, of which waited for: 1 -> 0; matrix products, arithmetic and copies ran while one was open for 1% -> 0% of each run, Pallas kernels for 0% -> 0%
where the time goes in v1:
time: 81.3 us; the launch traced here: 81.1 us
  Pallas kernels  77 us (95%)
  local copies, waits for them, and re-layouts  3.44 us (4%)
    pallas_call x1, Pallas kernels, local(): pl.pallas_call(functools.partial(kernel, Y, Z), out_shape=(jax.ShapeDtype...  77 us
    unnamed x9, local copies, waits for them, and re-layouts  3.42 us

profile of v1, /device:TPU:1, one launch (start us, length us, event | category | flops | bytes accessed | tf_op | source)
XLA Modules:
  0.0 81.1 jit_solution(3650825348957347074)
XLA Ops:
  0.6 0.0 copy-start
  0.6 1.3 %copy.7 = bf16[3,1,256,256]{2,3,0,1:T(8,128)(2,1)S(1)} copy(bf16[3,1,256,256]{3,2,1,0:T(8,128)(2,1)} %param.6) | data formatting | bytes 786432 | tf_op args[2]
  1.9 0.0 copy-start.1
  1.9 0.0 copy-start.2
  2.0 0.0 copy-done
  2.0 0.9 %copy-done.1 = bf16[3,1,256,256]{3,2,1,0:T(8,128)(2,1)S(1)} copy-done((bf16[3,1,256,256]{3,2,1,0:T(8,128)(2,1)S(1)}, bf16[3,1,256,256]{3,2,1,0:T(8,128)(2,1)}, u32[]{:S(2)}) %copy-start.1) | copy-done | bytes 393240
  2.9 0.0 copy-done.2
  2.9 77.0 %shard_map.59 = (bf16[2,4,16,256]{3,2,1,0:T(8,128)(2,1)S(1)}, f32[2,2]{1,0:T(2,128)S(1)}) custom-call(s32[3,4]{1,0:T(4,128)S(1)} %copy-done.2, bf16[2,4,256,256]{3,2,1,0:T(8,128)(2,1)S(1)} %bitcast.14, bf16[3,256,256]{2,1,0:T(8,128)(2,1)S(1)} %bitcast.15, bf16[4,3,64,256]{3,2,1,0:T(8,128)(2,1)S(1)} %bitcast.13), custom_call_target="tpu_custom_call" | custom-call | tf_op jit(solution)/shard_map/pallas_call | solution.py:301
  79.9 0.6 copy.14
  80.6 0.6 copy.15
  (1 shorter events, 0.0 us)
Async XLA Ops:
  0.6 1.3 %copy-start = (bf16[2,1,4,256,256]{4,3,2,1,0:T(8,128)(2,1)S(1)}, bf16[2,1,4,256,256]{4,3,2,1,0:T(8,128)(2,1)}, u32[]{:S(2)}) copy-start(bf16[2,1,4,256,256]{4,3,2,1,0:T(8,128)(2,1)} %param.4) | copy-start | bytes 3145732
  1.9 1.0 %copy-start.1 = (bf16[3,1,256,256]{3,2,1,0:T(8,128)(2,1)S(1)}, bf16[3,1,256,256]{3,2,1,0:T(8,128)(2,1)}, u32[]{:S(2)}) copy-start(bf16[3,1,256,256]{3,2,1,0:T(8,128)(2,1)} %param.5) | copy-start | bytes 1179652
  1.9 1.0 %copy-start.2 = (s32[3,4]{1,0:T(4,128)S(1)}, s32[3,4]{1,0:T(4,128)}, u32[]{:S(2)}) copy-start(s32[3,4]{1,0:T(4,128)} %off_ref.1) | copy-start | bytes 148

commit v2 on v0

v2 whole, which is shorter than its diff:
```python
import functools

import jax
import jax.numpy as jnp
from jax import lax
from jax.experimental import pallas as pl
from jax.experimental.pallas import tpu as pltpu
from jax.sharding import PartitionSpec as P

MESH = pl.DeviceIdType.MESH
X = 4
C = 2
H = 1
ORDER = (0, 3, 1, 2)
GROUPS = 18
ARRIVALS = 95


def kernel(Y, Z, off_ref, v_hbm, l_hbm, r_hbm, prod_ref, ray_ref,
           v_ref, l_ref, r_ref, rt, g0, g1, g2, lg, vg, inner, part, vcol, half, other,
           zsend, zgot, fin, fgot, gx, gk, gz, gy, load, send, recv):
    NI, PP, B, _ = v_ref.shape
    T = l_ref.shape[0]
    Q = B // X
    HQ = Q // H
    ZC = Z * C
    R = B // ZC
    PH = PP // C
    sec, term = lax.axis_index("sec"), lax.axis_index("term")
    x, y = sec // Y, sec % Y
    z, k = term // C, term % C
    w = z % 2
    f32, bf = jnp.float32, jnp.bfloat16

    def at(dx=0, dy=0, dz=0, dk=0):
        return (((x + dx) % X) * Y + (y + dy) % Y, ((z + dz) % Z) * C + (k + dk) % C)

    loads = [pltpu.make_async_copy(a, b, load.at[n]) for n, (a, b) in enumerate(
        ((r_hbm, r_ref), (v_hbm, v_ref), (l_hbm, l_ref)))]
    for made in loads:
        made.start()
    barrier = pltpu.get_barrier_semaphore()
    peers = [at(dx=d) for d in range(1, X)] + [at(dy=d) for d in range(1, Y)]
    peers += [at(dz=d) for d in range(1, Z)] + [at(dk=1)]
    for peer in peers:
        pl.semaphore_signal(barrier, inc=1, device_id=peer, device_id_type=MESH)
    loads[0].wait()
    for t in range(T):
        turned = r_ref[t].T
        for q in range(X):
            rt[q, t] = turned[q * Q:(q + 1) * Q]
    pieces = (g0, g1, g2)
    where = tuple((t, pl.ds(0, Q)) for t in range(T))
    for c, (t, rows) in enumerate(where):
        pieces[c][0] = rt[x, t, rows]
    loads[1].wait()
    loads[2].wait()
    pl.semaphore_wait(barrier, len(peers))

    used = []
    groups = {}

    def group(name):
        return groups.setdefault(name, len(groups))

    def fresh():
        used.append(0)
        return recv.at[len(used) - 1]

    def copy(src, dst, to, sent, got=None):
        made = pltpu.make_async_remote_copy(
            src_ref=src, dst_ref=dst, send_sem=send.at[group(sent)],
            recv_sem=fresh() if got is None else got,
            device_id=to, device_id_type=MESH)
        made.start()
        return made

    def drain(ref, sem):
        pltpu.make_async_copy(ref, ref, sem).wait()

    ring = {}

    def ring_send(c, d, first, count):
        g = pieces[c]
        for way in (1, -1):
            if 2 * d == Y and (first < X // 2) != (way == 1):
                continue
            ring[c, d, way, first, count] = copy(
                g.at[pl.ds(((-way * (d - 1)) % Y) * X + first, count)],
                g.at[pl.ds(((-way * d) % Y) * X + first, count)], at(dy=way), ("ring", c, way))

    def ring_pass(c, d):
        if 2 * d > Y:
            return
        for first in (0, 2):
            for key, made in list(ring.items()):
                if key[:2] == (c, d) and first <= key[3] < first + 2:
                    made.wait_recv()
            if 2 * d < Y:
                ring_send(c, d + 1, first, 2)

    rx = {}
    for c, (t, rows) in enumerate(where):
        got = None if c == 0 else fresh()
        for d in (1, 3, 2):
            rx[c, d] = copy(
                rt.at[(x + d) % X, t, rows], pieces[c].at[(-d) % X], at(dx=d), ("rx", c), got)
        rx[c] = got
        ring_send(c, 1, 0, 1)

    vx, vfwd, vz, vk, lx, lfwd = {}, {}, {}, {}, {}, {}

    def v_at(slot, i, n, core=k):
        return vg.at[(slot * NI + i) * PP + core * PH + n]

    for first in (0, 1):
        for way in (1, -1):
            n = first if way == 1 else 1 - first
            vx[way, n] = copy(v_ref.at[w, k * PH + n], v_at((-way) % X, w, n), at(dx=way), "v")

    def left_send(t):
        for way in (1, -1):
            lx[way, t] = copy(l_ref.at[t], lg.at[((-way) % X) * T + t], at(dx=way), "l")

    def left_pass(t):
        hb = B // 2
        for way in (1, -1):
            lx[way, t].wait_recv()
            rows = pl.ds(0 if way == 1 else hb, hb)
            lfwd[way, t] = copy(lg.at[((-way) % X) * T + t, rows], lg.at[2 * T + t, rows], at(dx=way), "l")

    def v_core_copy(slot, i, m, n):
        if (slot, m) not in vk:
            vk[slot, m] = fresh()
        copy(v_at(slot, i, n), v_at(slot, i, n), at(dk=1), "v", vk[slot, m])

    def v_share(slot, n):
        vz[slot, n] = copy(v_at(slot, w, n), v_at(slot, w, n), at(dz=-1 if n == 0 else 1), "v")
        v_core_copy(slot, w, 0, n)

    def v_pass(way, n):
        vx[way, n].wait_recv()
        slot = (-way) % X
        if (way, n) in ((1, 0), (-1, 1)):
            vfwd[n] = copy(v_at(slot, w, n), v_at(2, w, n), at(dx=way), "v")
        v_share(slot, n)

    def v_core(slot, n):
        vz[slot, n].wait_recv()
        v_core_copy(slot, 1 - w, 1, n)

    def v_wait(slot):
        for m in range(2):
            drain(vg.at[pl.ds(slot * NI * PP, PH)], vk[slot, m])

    def make_inner(o, t):
        d = ORDER[o]

        def body(p, carry):
            left = l_ref[t] if d == 0 else lg[d * T + t]
            for i in range(NI):
                v = v_ref[i, p] if d == 0 else vg[(d * NI + i) * PP + p]
                inner[o, t, p, i * B:(i + 1) * B] = jnp.dot(
                    left, v, preferred_element_type=f32).astype(bf)
            return carry

        lax.fori_loop(0, PP, body, 0)

    def make_columns(o):
        d = ORDER[o]
        for q in range(X):
            @pl.when(x == q)
            def _():
                def body(i, carry):
                    for p in range(PP):
                        for h in range(H):
                            cols = slice(q * Q + h * HQ, q * Q + (h + 1) * HQ)
                            v = v_ref[i, p, :, cols] if d == 0 else vg[(d * NI + i) * PP + p, :, cols]
                            vcol[h, o, i, :, :, p * HQ:(p + 1) * HQ] = v.reshape(ZC, R, HQ)
                    return carry

                lax.fori_loop(0, NI, body, 0)

    def outer(c, o):
        d = ORDER[o]
        t = where[c][0]
        for p in range(PP):
            off = off_ref[t, p]
            dy = off % Y
            dx = (d + off // Y + jnp.where(y + dy >= Y, 1, 0)) % X
            total = lax.dot_general(
                inner[o, t, p], pieces[c][dy * X + dx], (((1,), (1,)), ((), ())),
                preferred_element_type=f32)
            cols = slice(p * HQ, (p + 1) * HQ)
            for h in range(H):
                here = total[:, h * HQ:(h + 1) * HQ].reshape(NI, ZC, R, HQ)
                if c == 0:
                    part[h, o, :, :, :, cols] = here
                else:
                    part[h, o, :, :, :, cols] += here

    swap = {}
    zsem = [fresh() for h in range(H)]
    fsem = [fresh() for h in range(H)]

    def swap_send(h, o):
        for i in range(NI):
            for n in range(Z):
                half[h, o, i, n] = part[h, o, i, n * C + 1 - k].astype(bf)
        swap[h, o] = copy(half.at[h, o], other.at[h, o], at(dk=1), "swap")

    def swap_add(h, o):
        swap[h, o].wait_recv()
        for i in range(NI):
            for n in range(Z):
                total = part[h, o, i, n * C + k] + other[h, o, i, n].astype(f32)
                zsend[h, o, n, i] = total.astype(bf)
        for dz in sorted(range(1, Z), key=lambda d: -min(d, Z - d)):
            copy(zsend.at[h, o, (z + dz) % Z], zgot.at[h, ((-dz) % Z) * X + o], at(dz=dz), ("z", h), zsem[h])

    def gram_add(h, o, carry):
        def body(n, carry):
            out = list(carry)
            for i in range(NI):
                v = vcol[h, o, i, n].astype(f32)
                for j in range(NI):
                    out[i * NI + j] = out[i * NI + j] + v * part[h, o, j, n]
            return tuple(out)

        return lax.fori_loop(0, ZC, body, carry)

    def finish(h):
        drain(zgot.at[h, pl.ds(X, X * (Z - 1))], zsem[h])
        for o in range(X):
            for i in range(NI):
                total = zsend[h, o, z, i].astype(f32)
                for dz in range(1, Z):
                    total = total + zgot[h, dz * X + o, i].astype(f32)
                fin[h, o, i] = total.astype(bf)
            if o:
                copy(fin.at[h, o], fgot.at[h, x], at(dx=ORDER[o]), ("f", h), fsem[h])
        fgot[h, x] = fin[h, 0]

    def spread(buf, me, size, name):
        got = fresh()
        for d in range(1, size):
            copy(buf.at[me], buf.at[me], at(**{name: d}), name, got)
        return got

    def collect(buf, size, got):
        drain(buf.at[pl.ds(0, size - 1)], got)
        return jnp.sum(buf[...], axis=0)

    left_send(0)
    make_inner(0, 0)
    for d in (1, 3, 2):
        rx[0, d].wait_recv()
        ring_send(0, 1, (-d) % X, 1)
    make_inner(0, 1)
    for c in range(1, T):
        drain(pieces[c].at[pl.ds(1, X - 1)], rx[c])
        ring_send(c, 1, 1, 1)
        ring_send(c, 1, 2, 2)
    make_inner(0, 2)
    ring_pass(0, 1)
    v_pass(1, 0)
    v_pass(-1, 1)
    left_send(1)
    left_send(2)
    ring_pass(1, 1)
    make_columns(0)
    v_pass(1, 1)
    v_pass(-1, 0)
    ring_pass(0, 2)

    def squares(n, carry):
        rows = pl.ds(pl.multiple_of(n * 16, 16), 16)
        out = []
        for i in range(NI):
            total = carry[i]
            for p in range(PP):
                v = v_ref[i, p, rows].astype(f32)
                total = total + v * v
            out.append(total)
        return tuple(out)

    square = lax.fori_loop(0, B // 16, squares, (jnp.zeros((16, B), f32),) * NI)
    left_pass(0)
    ring_pass(1, 2)
    for slot in (3, 1):
        v_core(slot, 0)
        v_core(slot, 1)
    for n in range(PH):
        vfwd[n].wait_recv()
        v_share(2, n)
    ring_pass(2, 1)
    v_wait(3)
    make_inner(1, 0)
    ring_pass(0, 3)
    left_pass(1)
    make_inner(1, 1)
    ring_pass(1, 3)
    left_pass(2)
    make_inner(1, 2)
    v_core(2, 0)
    v_core(2, 1)
    v_wait(1)
    make_inner(2, 0)
    ring_pass(2, 2)
    make_inner(2, 1)
    ring_pass(0, 4)
    make_inner(2, 2)
    outer(0, 0)
    outer(0, 1)
    outer(0, 2)
    ring_pass(2, 3)
    ring_pass(1, 4)
    outer(1, 0)
    outer(1, 1)
    outer(1, 2)
    v_wait(2)
    for t in range(T):
        for way in (1, -1):
            lfwd[way, t].wait_recv()
        make_inner(3, t)
    outer(0, 3)
    outer(1, 3)
    ring_pass(2, 4)
    for o in range(X):
        outer(2, o)
        swap_send(0, o)
        if o:
            swap_add(0, o - 1)
    swap_add(0, 3)
    for o in range(1, X):
        make_columns(o)
    gram = (jnp.zeros((R, PP * HQ), f32),) * (NI * NI)
    for h in range(H):
        for o in range(X):
            gram = gram_add(h, o, gram)

    rows = [jnp.sum(g, axis=0, keepdims=True) for g in gram]
    W = rows[0].shape[1]
    for s in square:
        s = jnp.sum(s, axis=0, keepdims=True) * (1.0 / ZC)
        rows.append(sum(s[:, n * W:(n + 1) * W] for n in range(1, B // W)) + s[:, :W])
    for n in range(8):
        gk[k, n:n + 1] = rows[n] if n < len(rows) else jnp.zeros_like(rows[0])
    got_k = spread(gk, k, C, "dk")
    gx[x] = collect(gk, C, got_k)
    got_x = spread(gx, x, X, "dx")
    gy[y] = collect(gx, X, got_x)
    got_y = spread(gy, y, Y, "dy")
    gz[z] = collect(gy, Y, got_y)
    got_z = spread(gz, z, Z, "dz")
    finish(0)
    for h in range(H):
        drain(fgot.at[h, pl.ds(0, X - 1)], fsem[h])
    for q in range(X):
        for i in range(NI):
            for p in range(PP):
                prod_ref[i, p, :, q * Q:(q + 1) * Q] = jnp.concatenate(
                    [fgot[h, q, i, :, p * HQ:(p + 1) * HQ] for h in range(H)], axis=1)
    got = jnp.sum(collect(gz, Z, got_z), axis=1, keepdims=True)
    for i in range(NI):
        for j in range(NI):
            a = got[NI * NI + i:NI * NI + i + 1]
            b = got[NI * NI + j:NI * NI + j + 1]
            n = i * NI + j
            ray_ref[i:i + 1, j:j + 1] = got[n:n + 1] / jnp.sqrt(a * b)

    for c in range(T):
        for way in (1, -1):
            drain(pieces[c].at[pl.ds(0, X * (Y // 2 - 1) + X // 2)], send.at[group(("ring", c, way))])
        drain(pieces[c].at[pl.ds(0, X - 1)], send.at[group(("rx", c))])
    drain(vg.at[pl.ds(0, 24)], send.at[group("v")])
    drain(lg.at[pl.ds(0, 3 * T)], send.at[group("l")])
    drain(half, send.at[group("swap")])
    for h in range(H):
        drain(zgot.at[h, pl.ds(X, X * (Z - 1))], send.at[group(("z", h))])
        drain(fgot.at[h, pl.ds(0, X - 1)], send.at[group(("f", h))])
    for buf, size, name in ((gk, C, "dk"), (gx, X, "dx"), (gy, Y, "dy"), (gz, Z, "dz")):
        drain(buf.at[pl.ds(0, size - 1)], send.at[group(name)])
    assert len(used) <= recv.shape[0] and len(groups) <= send.shape[0], (len(used), len(groups))


def local(Y, Z, vectors, left_ops, right_ops, offsets):
    NI, _, PP, B, _ = vectors.shape
    T = left_ops.shape[0]
    Q, ZC = B // X, Z * C
    R, HQ = B // ZC, Q // H
    bf, f32 = jnp.bfloat16, jnp.float32
    vmem, dma = pltpu.VMEM, pltpu.SemaphoreType.DMA
    W = PP * HQ
    whole = pl.BlockSpec(memory_space=pltpu.VMEM)
    hbm = pl.BlockSpec(memory_space=pl.ANY)
    products, rayleigh = pl.pallas_call(
        functools.partial(kernel, Y, Z),
        out_shape=(jax.ShapeDtypeStruct((NI, PP, R, B), bf), jax.ShapeDtypeStruct((NI, NI), f32)),
        in_specs=[pl.BlockSpec(memory_space=pltpu.SMEM), hbm, hbm, hbm],
        out_specs=(whole, whole),
        scratch_shapes=[
            vmem((NI, PP, B, B), bf),
            vmem((T, B, B), bf),
            vmem((T, B, B), bf),
            vmem((X, T, Q, B), bf),
            vmem((Y * X, Q, B), bf),
            vmem((Y * X, Q, B), bf),
            vmem((Y * X, Q, B), bf),
            vmem((X * T, B, B), bf),
            vmem((X * NI * PP, B, B), bf),
            vmem((X, T, PP, NI * B, B), bf),
            vmem((H, X, NI, ZC, R, W), f32),
            vmem((H, X, NI, ZC, R, W), bf),
            vmem((H, X, NI, Z, R, W), bf),
            vmem((H, X, NI, Z, R, W), bf),
            vmem((H, X, Z, NI, R, W), bf),
            vmem((H, X * Z, NI, R, W), bf),
            vmem((H, X, NI, R, W), bf),
            vmem((H, X, NI, R, W), bf),
            vmem((X, 8, W), f32),
            vmem((C, 8, W), f32),
            vmem((Z, 8, W), f32),
            vmem((Y, 8, W), f32),
            dma((3,)),
            dma((GROUPS,)),
            dma((ARRIVALS,)),
        ],
        compiler_params=pltpu.CompilerParams(
            collective_id=0, has_side_effects=True, vmem_limit_bytes=56 * 1024 * 1024),
    )(offsets, vectors[:, 0], left_ops[:, 0], right_ops[:, 0])
    return products[:, None], rayleigh


def solution(mesh):
    sectors, terms = mesh.shape["sec"], mesh.shape["term"]
    in_specs = (
        P(None, "sec", None, None, None),
        P("term", "sec", None, None),
        P("term", "sec", None, None),
        P("term", None),
    )
    out_specs = (P(None, "sec", None, "term", None), P())
    return jax.shard_map(
        functools.partial(local, sectors // X, terms // C),
        mesh=mesh, in_specs=in_specs, out_specs=out_specs, check_vma=False)
```

time: 335 us -> 76.2 us (0.23)
  blocking collectives: 156 us -> 0 us
  waiting for transfers between devices: 130 us -> 0 us
  Pallas kernels: 0 us -> 73.3 us
  local copies, waits for them, and re-layouts: 27.3 us -> 2.04 us
  between operations: 14.9 us -> 0.65 us
  matrix products: 3.56 us -> 0 us
    all_gather x1 -> x0, waiting for transfers between devices: 130 us -> none  [local(): lax.all_gather(right_ops, 'sec', axis=1, tiled=True)]
    psum x1 -> x0, blocking collectives: 96.4 us -> none  [local(): gram_matrix, squares = lax.psum((gram_part, square_part), ('sec', 'term'))]
    pallas_call x0 -> x1, Pallas kernels: none -> 73.3 us  [local(): pl.pallas_call(functools.partial(kernel, Y, Z), out_shape=(jax.ShapeDtype...]
    unnamed x1 -> x0, blocking collectives: 59.1 us -> none
    gather x8 -> x0, local copies, waits for them, and re-layouts: 21.3 us -> none  [pick_blocks(): jnp.take_along_axis(piece, clipped[:, None, None, None], axis=1)[:, 0]]
    dot_general x2 -> x0, matrix products: 3.56 us -> none  [the longest x1 3.24 us: local(): jnp.einsum('tipac,ptcd->ipad', inner_part, picked, preferred_element_type...]
  transfers between devices with their start and end apart: 1 -> 0, of which waited for: 1 -> 0; matrix products, arithmetic and copies ran while one was open for 1% -> 0% of each run, Pallas kernels for 0% -> 0%
where the time goes in v2:
time: 76.2 us; the launch traced here: 76 us
  Pallas kernels  73.3 us (96%)
  local copies, waits for them, and re-layouts  2.04 us (3%)
    pallas_call x1, Pallas kernels, local(): pl.pallas_call(functools.partial(kernel, Y, Z), out_shape=(jax.ShapeDtype...  73.3 us
    unnamed x4, local copies, waits for them, and re-layouts  2.04 us

profile of v2, /device:TPU:1, one launch (start us, length us, event | category | flops | bytes accessed | tf_op | source)
XLA Modules:
  0.0 76.0 jit_solution(2756651881080500059)
XLA Ops:
  0.6 73.3 %shard_map.59 = (bf16[2,4,16,256]{3,2,1,0:T(8,128)(2,1)}, f32[2,2]{1,0:T(2,128)}) custom-call(s32[3,4]{1,0:T(4,128)} %off_ref.1, bf16[2,4,256,256]{3,2,1,0:T(8,128)(2,1)} %bitcast.6, bf16[3,256,256]{2,1,0:T(8,128)(2,1)} %bitcast.7, bf16[3,256,256]{2,1,0:T(8,128)(2,1)} %bitcast.8), custom_call_target="tpu_custom_call" | custom-call | tf_op jit(solution)/shard_map/pallas_call | solution.py:397
  73.9 0.0 copy-start
  73.9 1.5 %copy.9 = bf16[2,1,4,16,256]{4,3,2,1,0:T(8,128)(2,1)} copy(bf16[2,1,4,16,256]{4,3,2,1,0:T(8,128)(2,1)} %bitcast.9) | data formatting | bytes 131072
  75.4 0.0 copy-done
  75.4 0.6 copy.10
Async XLA Ops:
  73.9 1.5 %copy-start = (f32[2,2]{1,0:T(2,128)S(1)}, f32[2,2]{1,0:T(2,128)}, u32[]{:S(2)}) copy-start(f32[2,2]{1,0:T(2,128)} %get-tuple-element.11) | copy-start | bytes 52

commit v3 on v2

--- a/solution.py
+++ b/solution.py
@@ -287,26 +287,26 @@
     square = lax.fori_loop(0, B // 16, squares, (jnp.zeros((16, B), f32),) * NI)
     left_pass(0)
     ring_pass(1, 2)
+    ring_pass(2, 1)
     for slot in (3, 1):
         v_core(slot, 0)
         v_core(slot, 1)
+    v_wait(3)
+    make_inner(1, 0)
+    ring_pass(0, 3)
     for n in range(PH):
         vfwd[n].wait_recv()
         v_share(2, n)
-    ring_pass(2, 1)
-    v_wait(3)
-    make_inner(1, 0)
-    ring_pass(0, 3)
     left_pass(1)
     make_inner(1, 1)
     ring_pass(1, 3)
     left_pass(2)
     make_inner(1, 2)
+    ring_pass(2, 2)
+    v_wait(1)
+    make_inner(2, 0)
     v_core(2, 0)
     v_core(2, 1)
-    v_wait(1)
-    make_inner(2, 0)
-    ring_pass(2, 2)
     make_inner(2, 1)
     ring_pass(0, 4)
     make_inner(2, 2)

time: 76.2 us -> 75.7 us (level)
  no operation moved by 1% of the time
where the time goes in v3:
time: 75.7 us; the launch traced here: 75.4 us
  Pallas kernels  72.8 us (96%)
  local copies, waits for them, and re-layouts  2.04 us (3%)
    pallas_call x1, Pallas kernels, local(): pl.pallas_call(functools.partial(kernel, Y, Z), out_shape=(jax.ShapeDtype...  72.8 us
    unnamed x4, local copies, waits for them, and re-layouts  2.04 us

profile of v3, /device:TPU:1, one launch (start us, length us, event | category | flops | bytes accessed | tf_op | source)
XLA Modules:
  0.0 75.4 jit_solution(15602035149144463594)
XLA Ops:
  0.6 72.8 %shard_map.59 = (bf16[2,4,16,256]{3,2,1,0:T(8,128)(2,1)}, f32[2,2]{1,0:T(2,128)}) custom-call(s32[3,4]{1,0:T(4,128)} %off_ref.1, bf16[2,4,256,256]{3,2,1,0:T(8,128)(2,1)} %bitcast.6, bf16[3,256,256]{2,1,0:T(8,128)(2,1)} %bitcast.7, bf16[3,256,256]{2,1,0:T(8,128)(2,1)} %bitcast.8), custom_call_target="tpu_custom_call" | custom-call | tf_op jit(solution)/shard_map/pallas_call | solution.py:397
  73.4 0.0 copy-start
  73.4 1.5 %copy.9 = bf16[2,1,4,16,256]{4,3,2,1,0:T(8,128)(2,1)} copy(bf16[2,1,4,16,256]{4,3,2,1,0:T(8,128)(2,1)} %bitcast.9) | data formatting | bytes 131072
  74.9 0.0 copy-done
  74.9 0.6 copy.10
Async XLA Ops:
  73.4 1.5 %copy-start = (f32[2,2]{1,0:T(2,128)S(1)}, f32[2,2]{1,0:T(2,128)}, u32[]{:S(2)}) copy-start(f32[2,2]{1,0:T(2,128)} %get-tuple-element.11) | copy-start | bytes 52

commit v4 on v3

--- a/solution.py
+++ b/solution.py
@@ -329,8 +329,9 @@
     for o in range(X):
         outer(2, o)
         swap_send(0, o)
-        if o:
-            swap_add(0, o - 1)
+        if o > 1:
+            swap_add(0, o - 2)
+    swap_add(0, 2)
     swap_add(0, 3)
     for o in range(1, X):
         make_columns(o)

time: 75.7 us -> 75.9 us (level)
  no operation moved by 1% of the time
where the time goes in v4:
time: 75.9 us; the launch traced here: 75.7 us
  Pallas kernels  73 us (96%)
  local copies, waits for them, and re-layouts  2.04 us (3%)
    pallas_call x1, Pallas kernels, local(): pl.pallas_call(functools.partial(kernel, Y, Z), out_shape=(jax.ShapeDtype...  73 us
    unnamed x4, local copies, waits for them, and re-layouts  2.04 us

profile of v4, /device:TPU:1, one launch (start us, length us, event | category | flops | bytes accessed | tf_op | source)
XLA Modules:
  0.0 75.7 jit_solution(14471830689736052919)
XLA Ops:
  0.6 73.0 %shard_map.59 = (bf16[2,4,16,256]{3,2,1,0:T(8,128)(2,1)}, f32[2,2]{1,0:T(2,128)}) custom-call(s32[3,4]{1,0:T(4,128)} %off_ref.1, bf16[2,4,256,256]{3,2,1,0:T(8,128)(2,1)} %bitcast.6, bf16[3,256,256]{2,1,0:T(8,128)(2,1)} %bitcast.7, bf16[3,256,256]{2,1,0:T(8,128)(2,1)} %bitcast.8), custom_call_target="tpu_custom_call" | custom-call | tf_op jit(solution)/shard_map/pallas_call | solution.py:398
  73.6 0.0 copy-start
  73.6 1.5 %copy.9 = bf16[2,1,4,16,256]{4,3,2,1,0:T(8,128)(2,1)} copy(bf16[2,1,4,16,256]{4,3,2,1,0:T(8,128)(2,1)} %bitcast.9) | data formatting | bytes 131072
  75.1 0.0 copy-done
  75.1 0.6 copy.10
Async XLA Ops:
  73.6 1.5 %copy-start = (f32[2,2]{1,0:T(2,128)S(1)}, f32[2,2]{1,0:T(2,128)}, u32[]{:S(2)}) copy-start(f32[2,2]{1,0:T(2,128)} %get-tuple-element.11) | copy-start | bytes 52
